TPU v7x, 512 devices: a whole 4x8x8 slice. The times are simulated.
512 devices in a mesh: region: 16 (over y, core), tile: 32 (over x, z).
Axes of the slice: x: 4, y: 8, z: 8, core: 2. Of those that a mesh axis runs over, the one named last changes fastest.
Arguments:
- prior_pressure: float32 [64, 4, 64, 4096], P(None, None, 'region', 'tile'), may hold values from -6 to 6
- infiltration_source: float32 [64, 64, 4096], P(None, 'region', 'tile'), may hold values from -6 to 6
- soil_class: int32 [4, 64, 4096], P(None, 'region', 'tile'), may hold values from 0 to 11
- soil_k: float32 [12], replicated, may hold values from 0.02 to 0.2
- obs_index: int32 [131072], P(('region', 'tile')), may hold values from 0 to 2047
- obs_value: float32 [131072], P(('region', 'tile')), may hold values from -6 to 6
- obs_var: float32 [131072], P(('region', 'tile')), may hold values from 0.5 to 8
- obs_count: int32 [512], P(('region', 'tile')), may hold values from 1 to 256, as said below
Outputs:
- analysis: float32 [64, 4, 64, 4096], P(None, None, 'region', 'tile')
Inputs may be any that keep to these rules, and one draw needn't show every extreme that they name: `obs_count`: at least one block has all 256 slots live.
All inputs are finite; a program needn't handle non-finite values.
Results may differ from a plain program's by a relative error of at most 0.00019.
Values sent between devices are 32-bit elements; how exact they have to be, the bound alone decides.
No kernel may reach another device: no remote copies, remote signals or barrier semaphores. Data moves between devices by JAX's collectives and lax.ppermute only.
A program may use at most 64 MiB of HBM per device.

v0:
```python
import jax
import jax.numpy as jnp
from jax import lax
from jax.sharding import PartitionSpec as P

STEPS = 3
step_dt = 0.25
vert_share = 0.5


def extended(block, sides, width):
    for axis, dim in sides:
        count = lax.axis_size(axis)
        forward = [(i, i + 1) for i in range(count - 1)]
        backward = [(target, source) for source, target in forward]
        low = lax.ppermute(
            lax.slice_in_dim(block, block.shape[dim] - width, None, axis=dim), axis, forward
        )
        high = lax.ppermute(lax.slice_in_dim(block, 0, width, axis=dim), axis, backward)
        block = jnp.concatenate([low, block, high], axis=dim)
    return block


def lookup(soil_class, soil_k):
    total = jnp.zeros(soil_class.shape, jnp.float32)
    for index in range(soil_k.shape[0]):
        total = total + jnp.where(soil_class == index, soil_k[index], 0.0)
    return total


def cholesky_lower(matrix):
    order = matrix.shape[0]
    places = jnp.arange(order, dtype=jnp.int32)

    def column_step(column, lower):
        onehot = (places == column.astype(jnp.int32)).astype(matrix.dtype)
        row_now = jnp.dot(onehot, lower, precision=lax.Precision.HIGHEST)
        remain = jnp.dot(matrix, onehot, precision=lax.Precision.HIGHEST) - jnp.dot(
            lower, row_now, precision=lax.Precision.HIGHEST
        )
        pivot = jnp.sqrt(jnp.sum(remain * onehot))
        fresh = jnp.where(
            places >= column.astype(jnp.int32), remain / pivot, jnp.zeros_like(remain)
        )
        return lower + fresh[:, None] * onehot[None, :]

    return lax.fori_loop(0, order, column_step, jnp.zeros_like(matrix))


def lower_inverse(lower):
    order = lower.shape[0]
    places = jnp.arange(order, dtype=jnp.int32)

    def row_step(row, solved):
        onehot = (places == row.astype(jnp.int32)).astype(lower.dtype)
        row_now = jnp.dot(onehot, lower, precision=lax.Precision.HIGHEST)
        pivot = jnp.sum(row_now * onehot)
        fresh = (onehot - jnp.dot(row_now, solved, precision=lax.Precision.HIGHEST)) / pivot
        return solved + onehot[:, None] * fresh[None, :]

    return lax.fori_loop(0, order, row_step, jnp.zeros_like(lower))


def update(padded, bordered_permeability, push):
    cond = bordered_permeability[None] * (0.5 + jax.nn.sigmoid(padded))
    center = padded[:, :, 1:-1, 1:-1]
    kcen = cond[:, :, 1:-1, 1:-1]
    flux = jnp.zeros_like(center)
    for rows, cols in (
        (slice(2, None), slice(1, -1)),
        (slice(None, -2), slice(1, -1)),
        (slice(1, -1), slice(2, None)),
        (slice(1, -1), slice(None, -2)),
    ):
        flux = flux + 0.5 * (kcen + cond[:, :, rows, cols]) * (padded[:, :, rows, cols] - center)
    upward = vert_share * 0.5 * (kcen[:, 1:] + kcen[:, :-1]) * (center[:, 1:] - center[:, :-1])
    flux = (
        flux
        + jnp.pad(upward, ((0, 0), (0, 1), (0, 0), (0, 0)))
        - jnp.pad(upward, ((0, 0), (1, 0), (0, 0), (0, 0)))
    )
    flux = flux + jnp.pad(push[:, None], ((0, 0), (0, center.shape[1] - 1), (0, 0), (0, 0)))
    return center + step_dt * flux


def propagate_pressure(state, bordered_permeability, infiltration_source):
    padded = extended(state, (("region", 2), ("tile", 3)), 1)
    return update(padded, bordered_permeability, infiltration_source)


def shards(
    prior_pressure,
    infiltration_source,
    soil_class,
    soil_k,
    obs_index,
    obs_value,
    obs_var,
    obs_count,
):
    realization_vectors = prior_pressure.shape[0]
    depth = 1
    bordered_permeability = extended(
        lookup(soil_class, soil_k), (("region", 1), ("tile", 2)), depth
    )
    predicted_pressure = prior_pressure
    for step in range(STEPS):
        predicted_pressure = propagate_pressure(
            predicted_pressure, bordered_permeability, infiltration_source
        )
    unrolled_vector = predicted_pressure.reshape(realization_vectors, -1)
    measured_pressure = jnp.take(unrolled_vector, obs_index, axis=1)
    live = (jnp.arange(obs_index.shape[0], dtype=jnp.int32) < obs_count[0]).astype(jnp.float32)
    weight = live / jnp.sqrt(obs_var)
    hmean = jnp.mean(measured_pressure, axis=0)
    anomal = (measured_pressure - hmean) * weight
    innov = (obs_value - hmean) * weight
    gram = jnp.dot(anomal, anomal.T, precision=lax.Precision.HIGHEST)
    bvec = jnp.dot(anomal, innov, precision=lax.Precision.HIGHEST)
    eye = jnp.eye(realization_vectors, dtype=jnp.float32)
    gram, bvec = lax.psum((gram, bvec), ("region", "tile"))
    lower = cholesky_lower((realization_vectors - 1.0) * eye + gram)
    inverse = lower_inverse(lower)
    wmean = jnp.dot(
        inverse.T,
        jnp.dot(inverse, bvec, precision=lax.Precision.HIGHEST),
        precision=lax.Precision.HIGHEST,
    )
    wroot = inverse.T * jnp.sqrt(realization_vectors - 1.0)
    blending_factor = wroot + wmean[:, None]
    sample_average = jnp.mean(predicted_pressure, axis=0)
    deviation_matrix = (predicted_pressure - sample_average).reshape(realization_vectors, -1)
    propagated_vector = jnp.dot(
        blending_factor.T, deviation_matrix, precision=lax.Precision.HIGHEST
    ).reshape(predicted_pressure.shape)
    return sample_average + propagated_vector


def solution(mesh):
    return jax.shard_map(
        shards,
        mesh=mesh,
        in_specs=(
            P(None, None, "region", "tile"),
            P(None, "region", "tile"),
            P(None, "region", "tile"),
            P(),
            P(("region", "tile")),
            P(("region", "tile")),
            P(("region", "tile")),
            P(("region", "tile")),
        ),
        out_specs=P(None, None, "region", "tile"),
        check_vma=False,
    )
```

profile of v0, /device:TPU:1, one launch (start us, length us, event | category | flops | bytes accessed | tf_op | source)
XLA Modules:
  0.0 435.6 jit_solution(1766568834195470314)
XLA Ops:
  0.0 1.8 fusion.141
  1.8 8.3 %select_add_fusion.1 = f32[4,4,128]{2,1,0:T(4,128)S(1)} fusion(s32[4,4,128]{2,1,0:T(4,128)} %param.14, f32[]{:T(128)} %bitcast.11, f32[]{:T(128)} %bitcast.10, f32[]{:T(128)} %bitcast.9, f32[]{:T(128)} %bitcast.8, f32[]{:T(128)} %bitcast.7, f32[]{:T(128)} %bitcast.6, f32[]{:T(128)} %bitcast.5, f32[]{:T(128)} %bitcast.4, f32[]{:T(128)} %bitcast.3, ...), kind=kLoop, calls=%fused_computation.194 | loop fusion | flops 71680 | bytes 16432 | tf_op jit(solution)/shard_map/add | solution.py:27
  10.1 4.6 %collective-permute-start = (f32[4,1,128]{2,1,0:T(1,128)S(1)}, f32[4,1,128]{2,1,0:T(1,128)S(1)}, u32[]{:S(2)}, u32[]{:S(2)}) collective-permute-start(f32[4,1,128]{2,1,0:T(1,128)S(1)} %get-tuple-element.244), channel_id=1, source_target_pairs={{0,32},{32,64},{64,96},{96,128},{128,160},{160,192},{192,224},{224... | collective-permute-start | bytes 6152 | tf_op jit(solution)/shard_map/ppermute | solution.py:16
  14.7 5.5 %collective-permute-start.1 = (f32[4,1,128]{2,1,0:T(1,128)S(1)}, f32[4,1,128]{2,1,0:T(1,128)S(1)}, u32[]{:S(2)}, u32[]{:S(2)}) collective-permute-start(f32[4,1,128]{2,1,0:T(1,128)S(1)} %get-tuple-element.245), channel_id=1, source_target_pairs={{32,0},{64,32},{96,64},{128,96},{160,128},{192,160},{224,192},{256... | collective-permute-start | bytes 6152 | tf_op jit(solution)/shard_map/ppermute | solution.py:19
  20.2 1.2 copy.59
  21.4 1.9 collective-permute-start.4
  23.3 2.4 collective-permute-start.5
  26.5 2.3 collective-permute-start.2
  28.8 1.3 collective-permute-start.3
  32.0 4.1 collective-permute-start.6
  36.3 1.3 collective-permute-start.7
  38.8 2.6 collective-permute-done.7
  43.5 1.0 fusion.48
  44.5 5.1 %collective-permute-start.8 = (f32[64,4,1,128]{3,0,2,1:T(8,128)S(1)}, f32[64,4,1,128]{3,0,2,1:T(8,128)S(1)}, u32[]{:S(2)}, u32[]{:S(2)}) collective-permute-start(f32[64,4,1,128]{3,0,2,1:T(8,128)S(1)} %get-tuple-element.238), channel_id=1, source_target_pairs={{0,32},{32,64},{64,96},{96,128},{128,160},{160,192},{192,224},{224... | collective-permute-start | bytes 393224 | tf_op jit(solution)/shard_map/ppermute | solution.py:16
  49.6 1.9 collective-permute-start.9
  51.5 4.3 collective-permute-done.9
  56.6 5.2 %collective-permute-start.10 = (f32[64,4,6,1]{0,1,3,2:T(4,128)S(1)}, f32[64,4,6,1]{0,1,3,2:T(4,128)S(1)}, u32[]{:S(2)}, u32[]{:S(2)}) collective-permute-start(f32[64,4,6,1]{0,1,3,2:T(4,128)S(1)} %copy.60), channel_id=1, source_target_pairs={{0,1},{1,2},{2,3},{3,4},{4,5},{5,6},{6,7},{7,8},{8,9},{9,10},{10,1... | collective-permute-start | bytes 18440 | tf_op jit(solution)/shard_map/ppermute | solution.py:16
  62.1 1.3 collective-permute-start.11
  63.7 4.3 collective-permute-done.11
  69.4 1.0 fusion.50
  70.4 2.9 collective-permute-start.12
  73.4 1.9 collective-permute-start.13
  75.3 4.3 collective-permute-done.13
  80.3 4.9 %collective-permute-start.14 = (f32[64,4,6,1]{0,1,3,2:T(4,128)S(1)}, f32[64,4,6,1]{0,1,3,2:T(4,128)S(1)}, u32[]{:S(2)}, u32[]{:S(2)}) collective-permute-start(f32[64,4,6,1]{0,1,3,2:T(4,128)S(1)} %copy.66), channel_id=1, source_target_pairs={{0,1},{1,2},{2,3},{3,4},{4,5},{5,6},{6,7},{7,8},{8,9},{9,10},{10,1... | collective-permute-start | bytes 18440 | tf_op jit(solution)/shard_map/ppermute | solution.py:16
  85.5 1.3 collective-permute-start.15
  87.8 2.4 collective-permute-done.15
  91.5 1.1 fusion.131
  94.9 106.0 %all-reduce.7 = (f32[64,64]{1,0:T(8,128)S(1)}, f32[64]{0:T(128)S(1)}) all-reduce(f32[64,64]{1,0:T(8,128)S(1)} %fusion.112, f32[64]{0:T(128)S(1)} %convolution_bitcast_fusion.6), channel_id=1, replica_groups=mesh['region'=16,'tile'=32] {'region','tile'}, use_global_device_ids=true, to_apply=%region_2.3 | all-reduce | flops 4160 | bytes 33280 | tf_op jit(solution)/shard_map/psum | solution.py:121
  200.9 120.4 %while.30 = (s32[]{:T(128)}, f32[64,64]{1,0:T(8,128)S(1)}, f32[64,64]{1,0:T(8,128)S(1)}, s32[]{:T(128)}, s32[]{:T(128)}) while((s32[]{:T(128)}, f32[64,64]{1,0:T(8,128)S(1)}, f32[64,64]{1,0:T(8,128)S(1)}, s32[]{:T(128)}, s32[]{:T(128)}) %tuple.90), condition=%wide.region_5.6_spmd.clone.clone, body=%wide.region_3.5_spmd.clone.clone.sunk | while | flops 168642 | bytes 84589 | solution.py:47
  203.0 0.8 fusion.173
  204.9 0.8 fusion.173
  208.6 0.8 fusion.173
  210.5 0.8 fusion.173
  214.3 0.8 fusion.173
  216.2 0.8 fusion.173
  219.9 0.8 fusion.173
  221.8 0.8 fusion.173
  223.7 0.8 fusion.173
  225.6 0.8 fusion.173
  227.4 0.8 fusion.173
  229.3 0.8 fusion.173
  233.1 0.8 fusion.173
  235.0 0.8 fusion.173
  238.7 0.8 fusion.173
  240.6 0.8 fusion.173
  244.4 0.8 fusion.173
  246.3 0.8 fusion.173
  250.0 0.8 fusion.173
  251.9 0.8 fusion.173
  255.7 0.8 fusion.173
  257.5 0.8 fusion.173
  259.4 0.8 fusion.173
  261.3 0.8 fusion.173
  263.2 0.8 fusion.173
  265.1 0.8 fusion.173
  268.8 0.8 fusion.173
  270.7 0.8 fusion.173
  274.5 0.8 fusion.173
  276.3 0.8 fusion.173
  280.1 0.8 fusion.173
  282.0 0.8 fusion.173
  285.7 0.8 fusion.173
  321.2 111.2 %while.29 = (s32[]{:T(128)}, f32[64,64]{1,0:T(8,128)S(1)}, f32[64,64]{1,0:T(8,128)S(1)}, s32[]{:T(128)}, s32[]{:T(128)}) while((s32[]{:T(128)}, f32[64,64]{1,0:T(8,128)S(1)}, f32[64,64]{1,0:T(8,128)S(1)}, s32[]{:T(128)}, s32[]{:T(128)}) %tuple.93), condition=%wide.region_8.9_spmd.clone, body=%wide.region_6.8_spmd.clone.sunk | while | flops 115330 | bytes 67164 | solution.py:61
  434.5 1.1 copy.76
  (694 shorter events, 174.4 us)
Async XLA Ops:
  0.0 30.1 %copy-start = (f32[64,4,4,128]{3,2,1,0:T(4,128)S(1)}, f32[64,4,4,128]{3,2,1,0:T(4,128)}, u32[]{:S(2)}) copy-start(f32[64,4,4,128]{3,2,1,0:T(4,128)} %param.12) | copy-start | bytes 1572868
  0.0 25.8 %copy-start.7 = (f32[64,4,128]{2,1,0:T(4,128)S(1)}, f32[64,4,128]{2,1,0:T(4,128)}, u32[]{:S(2)}) copy-start(f32[64,4,128]{2,1,0:T(4,128)} %param.13) | copy-start | bytes 393220
  10.1 15.7 %collective-permute-start = (f32[4,1,128]{2,1,0:T(1,128)S(1)}, f32[4,1,128]{2,1,0:T(1,128)S(1)}, u32[]{:S(2)}, u32[]{:S(2)}) collective-permute-start(f32[4,1,128]{2,1,0:T(1,128)S(1)} %get-tuple-element.244), channel_id=1, source_target_pairs={{0,32},{32,64},{64,96},{96,128},{128,160},{160,192},{192,224},{224... | collective-permute-start | bytes 6152 | tf_op jit(solution)/shard_map/ppermute | solution.py:16
  14.7 11.1 %collective-permute-start.1 = (f32[4,1,128]{2,1,0:T(1,128)S(1)}, f32[4,1,128]{2,1,0:T(1,128)S(1)}, u32[]{:S(2)}, u32[]{:S(2)}) collective-permute-start(f32[4,1,128]{2,1,0:T(1,128)S(1)} %get-tuple-element.245), channel_id=1, source_target_pairs={{32,0},{64,32},{96,64},{128,96},{160,128},{192,160},{224,192},{256... | collective-permute-start | bytes 6152 | tf_op jit(solution)/shard_map/ppermute | solution.py:19
  21.4 8.6 %collective-permute-start.4 = (f32[64,4,1,128]{3,0,2,1:T(8,128)S(1)}, f32[64,4,1,128]{3,0,2,1:T(8,128)S(1)}, u32[]{:S(2)}, u32[]{:S(2)}) collective-permute-start(f32[64,4,1,128]{3,0,2,1:T(8,128)S(1)} %get-tuple-element.241), channel_id=1, source_target_pairs={{0,32},{32,64},{64,96},{96,128},{128,160},{160,192},{192,224},{224... | collective-permute-start | bytes 393224 | tf_op jit(solution)/shard_map/ppermute | solution.py:16
  23.3 6.9 %collective-permute-start.5 = (f32[64,4,1,128]{3,0,2,1:T(8,128)S(1)}, f32[64,4,1,128]{3,0,2,1:T(8,128)S(1)}, u32[]{:S(2)}, u32[]{:S(2)}) collective-permute-start(f32[64,4,1,128]{3,0,2,1:T(8,128)S(1)} %get-tuple-element.240), channel_id=1, source_target_pairs={{32,0},{64,32},{96,64},{128,96},{160,128},{192,160},{224,192},{256... | collective-permute-start | bytes 393224 | tf_op jit(solution)/shard_map/ppermute | solution.py:19
  26.5 11.1 %collective-permute-start.2 = (f32[4,6,1]{2,1,0:T(8,128)}, f32[4,6,1]{2,1,0:T(8,128)}, u32[]{:S(2)}, u32[]{:S(2)}) collective-permute-start(f32[4,6,1]{2,1,0:T(8,128)} %get-tuple-element.242), channel_id=1, source_target_pairs={{0,1},{1,2},{2,3},{3,4},{4,5},{5,6},{6,7},{7,8},{8,9},{9,10},{10,1... | collective-permute-start | bytes 296 | tf_op jit(solution)/shard_map/ppermute | solution.py:16
  28.8 8.9 %collective-permute-start.3 = (f32[4,6,1]{2,1,0:T(8,128)}, f32[4,6,1]{2,1,0:T(8,128)}, u32[]{:S(2)}, u32[]{:S(2)}) collective-permute-start(f32[4,6,1]{2,1,0:T(8,128)} %get-tuple-element.243), channel_id=1, source_target_pairs={{1,0},{2,1},{3,2},{4,3},{5,4},{6,5},{7,6},{8,7},{9,8},{10,9},{11,1... | collective-permute-start | bytes 296 | tf_op jit(solution)/shard_map/ppermute | solution.py:19
  30.1 0.7 copy-start.3
  30.7 0.7 copy-start.5
  32.0 6.5 %collective-permute-start.6 = (f32[64,4,6,1]{0,1,3,2:T(4,128)S(1)}, f32[64,4,6,1]{0,1,3,2:T(4,128)S(1)}, u32[]{:S(2)}, u32[]{:S(2)}) collective-permute-start(f32[64,4,6,1]{0,1,3,2:T(4,128)S(1)} %copy.44), channel_id=1, source_target_pairs={{0,1},{1,2},{2,3},{3,4},{4,5},{5,6},{6,7},{7,8},{8,9},{9,10},{10,1... | collective-permute-start | bytes 18440 | tf_op jit(solution)/shard_map/ppermute | solution.py:16
  36.3 5.1 %collective-permute-start.7 = (f32[64,4,6,1]{0,1,3,2:T(4,128)S(1)}, f32[64,4,6,1]{0,1,3,2:T(4,128)S(1)}, u32[]{:S(2)}, u32[]{:S(2)}) collective-permute-start(f32[64,4,6,1]{0,1,3,2:T(4,128)S(1)} %copy.45), channel_id=1, source_target_pairs={{1,0},{2,1},{3,2},{4,3},{5,4},{6,5},{7,6},{8,7},{9,8},{10,9},{11,1... | collective-permute-start | bytes 18440 | tf_op jit(solution)/shard_map/ppermute | solution.py:19
  38.5 4.0 copy-start.1
  42.5 0.9 copy-start.4
  42.5 1.0 copy-start.6
  44.5 7.0 %collective-permute-start.8 = (f32[64,4,1,128]{3,0,2,1:T(8,128)S(1)}, f32[64,4,1,128]{3,0,2,1:T(8,128)S(1)}, u32[]{:S(2)}, u32[]{:S(2)}) collective-permute-start(f32[64,4,1,128]{3,0,2,1:T(8,128)S(1)} %get-tuple-element.238), channel_id=1, source_target_pairs={{0,32},{32,64},{64,96},{96,128},{128,160},{160,192},{192,224},{224... | collective-permute-start | bytes 393224 | tf_op jit(solution)/shard_map/ppermute | solution.py:16
  49.6 6.3 %collective-permute-start.9 = (f32[64,4,1,128]{3,0,2,1:T(8,128)S(1)}, f32[64,4,1,128]{3,0,2,1:T(8,128)S(1)}, u32[]{:S(2)}, u32[]{:S(2)}) collective-permute-start(f32[64,4,1,128]{3,0,2,1:T(8,128)S(1)} %get-tuple-element.239), channel_id=1, source_target_pairs={{32,0},{64,32},{96,64},{128,96},{160,128},{192,160},{224,192},{256... | collective-permute-start | bytes 393224 | tf_op jit(solution)/shard_map/ppermute | solution.py:19
  56.3 7.1 %copy-start.8 = (s32[256]{0:T(256)S(1)}, s32[256]{0:T(256)}, u32[]{:S(2)}) copy-start(s32[256]{0:T(256)} %param.16) | copy-start | bytes 3076
  56.3 12.1 %copy-start.2 = (f32[4,6,130]{2,1,0:T(8,128)S(1)}, f32[4,6,130]{2,1,0:T(8,128)}, u32[]{:S(2)}) copy-start(f32[4,6,130]{2,1,0:T(8,128)} %copy-done.1) | copy-start | bytes 37444
  56.6 6.8 %collective-permute-start.10 = (f32[64,4,6,1]{0,1,3,2:T(4,128)S(1)}, f32[64,4,6,1]{0,1,3,2:T(4,128)S(1)}, u32[]{:S(2)}, u32[]{:S(2)}) collective-permute-start(f32[64,4,6,1]{0,1,3,2:T(4,128)S(1)} %copy.60), channel_id=1, source_target_pairs={{0,1},{1,2},{2,3},{3,4},{4,5},{5,6},{6,7},{7,8},{8,9},{9,10},{10,1... | collective-permute-start | bytes 18440 | tf_op jit(solution)/shard_map/ppermute | solution.py:16
  62.1 5.9 %collective-permute-start.11 = (f32[64,4,6,1]{0,1,3,2:T(4,128)S(1)}, f32[64,4,6,1]{0,1,3,2:T(4,128)S(1)}, u32[]{:S(2)}, u32[]{:S(2)}) collective-permute-start(f32[64,4,6,1]{0,1,3,2:T(4,128)S(1)} %copy.61), channel_id=1, source_target_pairs={{1,0},{2,1},{3,2},{4,3},{5,4},{6,5},{7,6},{8,7},{9,8},{10,9},{11,1... | collective-permute-start | bytes 18440 | tf_op jit(solution)/shard_map/ppermute | solution.py:19
  70.4 4.9 %collective-permute-start.12 = (f32[64,4,1,128]{3,0,2,1:T(8,128)S(1)}, f32[64,4,1,128]{3,0,2,1:T(8,128)S(1)}, u32[]{:S(2)}, u32[]{:S(2)}) collective-permute-start(f32[64,4,1,128]{3,0,2,1:T(8,128)S(1)} %get-tuple-element.236), channel_id=1, source_target_pairs={{0,32},{32,64},{64,96},{96,128},{128,160},{160,192},{192,224},{224... | collective-permute-start | bytes 393224 | tf_op jit(solution)/shard_map/ppermute | solution.py:16
  73.4 6.3 %collective-permute-start.13 = (f32[64,4,1,128]{3,0,2,1:T(8,128)S(1)}, f32[64,4,1,128]{3,0,2,1:T(8,128)S(1)}, u32[]{:S(2)}, u32[]{:S(2)}) collective-permute-start(f32[64,4,1,128]{3,0,2,1:T(8,128)S(1)} %get-tuple-element.237), channel_id=1, source_target_pairs={{32,0},{64,32},{96,64},{128,96},{160,128},{192,160},{224,192},{256... | collective-permute-start | bytes 393224 | tf_op jit(solution)/shard_map/ppermute | solution.py:19
  80.3 7.1 %collective-permute-start.14 = (f32[64,4,6,1]{0,1,3,2:T(4,128)S(1)}, f32[64,4,6,1]{0,1,3,2:T(4,128)S(1)}, u32[]{:S(2)}, u32[]{:S(2)}) collective-permute-start(f32[64,4,6,1]{0,1,3,2:T(4,128)S(1)} %copy.66), channel_id=1, source_target_pairs={{0,1},{1,2},{2,3},{3,4},{4,5},{5,6},{6,7},{7,8},{8,9},{9,10},{10,1... | collective-permute-start | bytes 18440 | tf_op jit(solution)/shard_map/ppermute | solution.py:16
  85.5 4.7 %collective-permute-start.15 = (f32[64,4,6,1]{0,1,3,2:T(4,128)S(1)}, f32[64,4,6,1]{0,1,3,2:T(4,128)S(1)}, u32[]{:S(2)}, u32[]{:S(2)}) collective-permute-start(f32[64,4,6,1]{0,1,3,2:T(4,128)S(1)} %copy.67), channel_id=1, source_target_pairs={{1,0},{2,1},{3,2},{4,3},{5,4},{6,5},{7,6},{8,7},{9,8},{10,9},{11,1... | collective-permute-start | bytes 18440 | tf_op jit(solution)/shard_map/ppermute | solution.py:19
  92.6 1.3 copy-start.9
  92.6 1.3 copy-start.10
where the time goes:
time: 441 us; the launch traced here: 436 us
  matrix products  178 us (40%)
  blocking collectives  106 us (24%)
  starting transfers between devices  47.8 us (11%)
  loops' own time  45.1 us (10%)
  other arithmetic  26.4 us (6%)
  waiting for transfers between devices  18 us (4%)
  local copies, waits for them, and re-layouts  13.4 us (3%)
    psum x1, blocking collectives, shards(): gram, bvec = lax.psum((gram, bvec), ('region', 'tile'))  106 us
    dot_general x64, matrix products, column_step(): jnp.dot(lower, row_now, precision=lax.Precision.HIGHEST)  53.6 us
    dot_general x64, matrix products, row_step(): row_now = jnp.dot(onehot, lower, precision=lax.Precision.HIGHEST)  52.8 us
    dot_general x64, matrix products, row_step(): jnp.dot(row_now, solved, precision=lax.Precision.HIGHEST)  52.7 us
    another operation x1, loops' own time, cholesky_lower(): return lax.fori_loop(0, order, column_step, jnp.zeros_like(matrix))  44.6 us
    ppermute x8, starting transfers between devices, extended(): lax.ppermute(lax.slice_in_dim(block, block.shape[dim] - width, None, axis...  30.9 us
    ppermute x8, waiting for transfers between devices, extended(): lax.ppermute(lax.slice_in_dim(block, 0, width, axis=dim), axis, backward)  17.9 us
    ppermute x8, starting transfers between devices, extended(): lax.ppermute(lax.slice_in_dim(block, 0, width, axis=dim), axis, backward)  16.9 us
  transfers between devices with their start and end apart: 16, of which 5 were waited for; matrix products, arithmetic and copies ran while one was open for 1% of the time, Pallas kernels for 0%

commit v1 on v0

--- a/solution.py
+++ b/solution.py
@@ -6,6 +6,11 @@
 STEPS = 3
 step_dt = 0.25
 vert_share = 0.5
+
+
+def axis_by_axis(value, one, other):
+    partial = lax.psum(value, one)
+    return lax.psum(partial, other)
 
 
 def extended(block, sides, width):
@@ -118,7 +123,7 @@
     gram = jnp.dot(anomal, anomal.T, precision=lax.Precision.HIGHEST)
     bvec = jnp.dot(anomal, innov, precision=lax.Precision.HIGHEST)
     eye = jnp.eye(realization_vectors, dtype=jnp.float32)
-    gram, bvec = lax.psum((gram, bvec), ("region", "tile"))
+    gram, bvec = axis_by_axis((gram, bvec), "tile", "region")
     lower = cholesky_lower((realization_vectors - 1.0) * eye + gram)
     inverse = lower_inverse(lower)
     wmean = jnp.dot(

time: 441 us -> 513 us (1.16)
  blocking collectives: 106 us -> 184 us
  matrix products: 178 us -> 168 us
    psum x1 -> x2, blocking collectives: 106 us -> 184 us  [the longest x1 112 us: axis_by_axis(): partial = lax.psum(value, one)]
    dot_general x64, matrix products: 52.7 us -> 45.2 us  [row_step(): jnp.dot(row_now, solved, precision=lax.Precision.HIGHEST)]
where the time goes in v1:
time: 513 us; the launch traced here: 506 us
  blocking collectives  184 us (36%)
  matrix products  168 us (33%)
  starting transfers between devices  47.8 us (9%)
  loops' own time  47.6 us (9%)
  other arithmetic  26.4 us (5%)
  waiting for transfers between devices  18 us (4%)
  local copies, waits for them, and re-layouts  13.4 us (3%)
    psum x1, blocking collectives, axis_by_axis(): partial = lax.psum(value, one)  112 us
    psum x1, blocking collectives, axis_by_axis(): return lax.psum(partial, other)  71.8 us
    dot_general x64, matrix products, column_step(): jnp.dot(lower, row_now, precision=lax.Precision.HIGHEST)  56.3 us
    dot_general x64, matrix products, row_step(): row_now = jnp.dot(onehot, lower, precision=lax.Precision.HIGHEST)  47.9 us
    another operation x1, loops' own time, cholesky_lower(): return lax.fori_loop(0, order, column_step, jnp.zeros_like(matrix))  47.2 us
    dot_general x64, matrix products, row_step(): jnp.dot(row_now, solved, precision=lax.Precision.HIGHEST)  45.2 us
    ppermute x8, starting transfers between devices, extended(): lax.ppermute(lax.slice_in_dim(block, block.shape[dim] - width, None, axis...  30.9 us
    ppermute x8, waiting for transfers between devices, extended(): lax.ppermute(lax.slice_in_dim(block, 0, width, axis=dim), axis, backward)  17.9 us
  transfers between devices with their start and end apart: 16, of which 5 were waited for; matrix products, arithmetic and copies ran while one was open for 1% of the time, Pallas kernels for 0%

profile of v1, /device:TPU:1, one launch (start us, length us, event | category | flops | bytes accessed | tf_op | source)
XLA Modules:
  0.0 506.3 jit_solution(924067659822047134)
XLA Ops:
  0.0 1.8 fusion.141
  1.8 8.3 %select_add_fusion.1 = f32[4,4,128]{2,1,0:T(4,128)S(1)} fusion(s32[4,4,128]{2,1,0:T(4,128)} %param.14, f32[]{:T(128)} %bitcast.11, f32[]{:T(128)} %bitcast.10, f32[]{:T(128)} %bitcast.9, f32[]{:T(128)} %bitcast.8, f32[]{:T(128)} %bitcast.7, f32[]{:T(128)} %bitcast.6, f32[]{:T(128)} %bitcast.5, f32[]{:T(128)} %bitcast.4, f32[]{:T(128)} %bitcast.3, ...), kind=kLoop, calls=%fused_computation.194 | loop fusion | flops 71680 | bytes 16432 | tf_op jit(solution)/shard_map/add | solution.py:32
  10.1 4.6 collective-permute-start
  14.7 5.5 %collective-permute-start.1 = (f32[4,1,128]{2,1,0:T(1,128)S(1)}, f32[4,1,128]{2,1,0:T(1,128)S(1)}, u32[]{:S(2)}, u32[]{:S(2)}) collective-permute-start(f32[4,1,128]{2,1,0:T(1,128)S(1)} %get-tuple-element.247), channel_id=1, source_target_pairs={{32,0},{64,32},{96,64},{128,96},{160,128},{192,160},{224,192},{256... | collective-permute-start | bytes 6152 | tf_op jit(solution)/shard_map/ppermute | solution.py:24
  20.2 1.2 copy.59
  21.4 1.9 collective-permute-start.4
  23.3 2.4 collective-permute-start.5
  26.5 2.3 collective-permute-start.2
  28.8 1.3 collective-permute-start.3
  32.0 4.1 collective-permute-start.6
  36.3 1.3 collective-permute-start.7
  38.8 2.6 collective-permute-done.7
  43.4 1.0 fusion.48
  44.5 5.1 %collective-permute-start.8 = (f32[64,4,1,128]{3,0,2,1:T(8,128)S(1)}, f32[64,4,1,128]{3,0,2,1:T(8,128)S(1)}, u32[]{:S(2)}, u32[]{:S(2)}) collective-permute-start(f32[64,4,1,128]{3,0,2,1:T(8,128)S(1)} %get-tuple-element.240), channel_id=1, source_target_pairs={{0,32},{32,64},{64,96},{96,128},{128,160},{160,192},{192,224},{224... | collective-permute-start | bytes 393224 | tf_op jit(solution)/shard_map/ppermute | solution.py:21
  49.6 1.9 collective-permute-start.9
  51.5 4.3 collective-permute-done.9
  56.6 5.2 %collective-permute-start.10 = (f32[64,4,6,1]{0,1,3,2:T(4,128)S(1)}, f32[64,4,6,1]{0,1,3,2:T(4,128)S(1)}, u32[]{:S(2)}, u32[]{:S(2)}) collective-permute-start(f32[64,4,6,1]{0,1,3,2:T(4,128)S(1)} %copy.60), channel_id=1, source_target_pairs={{0,1},{1,2},{2,3},{3,4},{4,5},{5,6},{6,7},{7,8},{8,9},{9,10},{10,1... | collective-permute-start | bytes 18440 | tf_op jit(solution)/shard_map/ppermute | solution.py:21
  62.1 1.3 collective-permute-start.11
  63.7 4.3 collective-permute-done.11
  69.3 1.0 fusion.50
  70.4 2.9 collective-permute-start.12
  73.4 1.9 collective-permute-start.13
  75.3 4.3 collective-permute-done.13
  80.3 4.9 collective-permute-start.14
  85.5 1.3 collective-permute-start.15
  87.8 2.4 collective-permute-done.15
  91.5 1.1 fusion.131
  94.9 112.0 %all-reduce.7 = (f32[64,64]{1,0:T(8,128)S(1)}, f32[64]{0:T(128)S(1)}) all-reduce(f32[64,64]{1,0:T(8,128)S(1)} %fusion.112, f32[64]{0:T(128)S(1)} %convolution_bitcast_fusion.6), channel_id=1, replica_groups=mesh['region'=16,'tile'=32] {'tile'}, use_global_device_ids=true, to_apply=%region_2.3 | all-reduce | flops 4160 | bytes 33280 | tf_op jit(solution)/shard_map/psum | solution.py:12
  206.9 71.8 %all-reduce.8 = (f32[64,64]{1,0:T(8,128)S(1)}, f32[64]{0:T(128)S(1)}) all-reduce(f32[64,64]{1,0:T(8,128)S(1)} %get-tuple-element.220, f32[64]{0:T(128)S(1)} %get-tuple-element.221), channel_id=1, replica_groups=mesh['region'=16,'tile'=32] {'region'}, use_global_device_ids=true, to_apply=%region_3.4 | all-reduce | flops 4160 | bytes 33280 | tf_op jit(solution)/shard_map/psum | solution.py:13
  278.7 125.6 %while.30 = (s32[]{:T(128)}, f32[64,64]{1,0:T(8,128)S(1)}, f32[64,64]{1,0:T(8,128)S(1)}, s32[]{:T(128)}, s32[]{:T(128)}) while((s32[]{:T(128)}, f32[64,64]{1,0:T(8,128)S(1)}, f32[64,64]{1,0:T(8,128)S(1)}, s32[]{:T(128)}, s32[]{:T(128)}) %tuple.90), condition=%wide.region_6.7_spmd.clone.clone, body=%wide.region_4.6_spmd.clone.clone.sunk | while | flops 168642 | bytes 84589 | solution.py:52
  279.0 0.9 fusion.173
  280.9 0.9 fusion.173
  282.9 0.9 fusion.173
  284.9 0.9 fusion.173
  286.8 0.9 fusion.173
  288.8 0.9 fusion.173
  290.8 0.9 fusion.173
  292.7 0.9 fusion.173
  294.7 0.9 fusion.173
  296.6 0.9 fusion.173
  298.6 0.9 fusion.173
  300.6 0.9 fusion.173
  304.5 0.9 fusion.173
  310.4 0.9 fusion.173
  312.3 0.9 fusion.173
  318.2 0.9 fusion.173
  320.2 0.9 fusion.173
  326.1 0.9 fusion.173
  333.9 0.9 fusion.173
  341.8 0.9 fusion.173
  347.7 0.9 fusion.173
  349.6 0.9 fusion.173
  355.5 0.9 fusion.173
  357.5 0.9 fusion.173
  363.4 0.9 fusion.173
  371.2 0.9 fusion.173
  379.1 0.9 fusion.173
  384.9 0.9 fusion.173
  386.9 0.9 fusion.173
  392.8 0.9 fusion.173
  394.7 0.9 fusion.173
  400.6 0.9 fusion.173
  404.3 98.8 %while.29 = (s32[]{:T(128)}, f32[64,64]{1,0:T(8,128)S(1)}, f32[64,64]{1,0:T(8,128)S(1)}, s32[]{:T(128)}, s32[]{:T(128)}) while((s32[]{:T(128)}, f32[64,64]{1,0:T(8,128)S(1)}, f32[64,64]{1,0:T(8,128)S(1)}, s32[]{:T(128)}, s32[]{:T(128)}) %tuple.93), condition=%wide.region_9.10_spmd.clone, body=%wide.region_7.9_spmd.clone.sunk | while | flops 115330 | bytes 67164 | solution.py:66
  505.1 1.1 copy.76
  (695 shorter events, 164.1 us)
Async XLA Ops:
  0.0 30.1 %copy-start = (f32[64,4,4,128]{3,2,1,0:T(4,128)S(1)}, f32[64,4,4,128]{3,2,1,0:T(4,128)}, u32[]{:S(2)}) copy-start(f32[64,4,4,128]{3,2,1,0:T(4,128)} %param.12) | copy-start | bytes 1572868
  0.0 25.8 %copy-start.7 = (f32[64,4,128]{2,1,0:T(4,128)S(1)}, f32[64,4,128]{2,1,0:T(4,128)}, u32[]{:S(2)}) copy-start(f32[64,4,128]{2,1,0:T(4,128)} %param.13) | copy-start | bytes 393220
  10.1 15.7 %collective-permute-start = (f32[4,1,128]{2,1,0:T(1,128)S(1)}, f32[4,1,128]{2,1,0:T(1,128)S(1)}, u32[]{:S(2)}, u32[]{:S(2)}) collective-permute-start(f32[4,1,128]{2,1,0:T(1,128)S(1)} %get-tuple-element.246), channel_id=1, source_target_pairs={{0,32},{32,64},{64,96},{96,128},{128,160},{160,192},{192,224},{224... | collective-permute-start | bytes 6152 | tf_op jit(solution)/shard_map/ppermute | solution.py:21
  14.7 11.1 %collective-permute-start.1 = (f32[4,1,128]{2,1,0:T(1,128)S(1)}, f32[4,1,128]{2,1,0:T(1,128)S(1)}, u32[]{:S(2)}, u32[]{:S(2)}) collective-permute-start(f32[4,1,128]{2,1,0:T(1,128)S(1)} %get-tuple-element.247), channel_id=1, source_target_pairs={{32,0},{64,32},{96,64},{128,96},{160,128},{192,160},{224,192},{256... | collective-permute-start | bytes 6152 | tf_op jit(solution)/shard_map/ppermute | solution.py:24
  21.4 8.6 %collective-permute-start.4 = (f32[64,4,1,128]{3,0,2,1:T(8,128)S(1)}, f32[64,4,1,128]{3,0,2,1:T(8,128)S(1)}, u32[]{:S(2)}, u32[]{:S(2)}) collective-permute-start(f32[64,4,1,128]{3,0,2,1:T(8,128)S(1)} %get-tuple-element.243), channel_id=1, source_target_pairs={{0,32},{32,64},{64,96},{96,128},{128,160},{160,192},{192,224},{224... | collective-permute-start | bytes 393224 | tf_op jit(solution)/shard_map/ppermute | solution.py:21
  23.3 6.9 %collective-permute-start.5 = (f32[64,4,1,128]{3,0,2,1:T(8,128)S(1)}, f32[64,4,1,128]{3,0,2,1:T(8,128)S(1)}, u32[]{:S(2)}, u32[]{:S(2)}) collective-permute-start(f32[64,4,1,128]{3,0,2,1:T(8,128)S(1)} %get-tuple-element.242), channel_id=1, source_target_pairs={{32,0},{64,32},{96,64},{128,96},{160,128},{192,160},{224,192},{256... | collective-permute-start | bytes 393224 | tf_op jit(solution)/shard_map/ppermute | solution.py:24
  26.5 11.1 %collective-permute-start.2 = (f32[4,6,1]{2,1,0:T(8,128)}, f32[4,6,1]{2,1,0:T(8,128)}, u32[]{:S(2)}, u32[]{:S(2)}) collective-permute-start(f32[4,6,1]{2,1,0:T(8,128)} %get-tuple-element.244), channel_id=1, source_target_pairs={{0,1},{1,2},{2,3},{3,4},{4,5},{5,6},{6,7},{7,8},{8,9},{9,10},{10,1... | collective-permute-start | bytes 296 | tf_op jit(solution)/shard_map/ppermute | solution.py:21
  28.8 8.9 %collective-permute-start.3 = (f32[4,6,1]{2,1,0:T(8,128)}, f32[4,6,1]{2,1,0:T(8,128)}, u32[]{:S(2)}, u32[]{:S(2)}) collective-permute-start(f32[4,6,1]{2,1,0:T(8,128)} %get-tuple-element.245), channel_id=1, source_target_pairs={{1,0},{2,1},{3,2},{4,3},{5,4},{6,5},{7,6},{8,7},{9,8},{10,9},{11,1... | collective-permute-start | bytes 296 | tf_op jit(solution)/shard_map/ppermute | solution.py:24
  30.1 0.7 copy-start.3
  30.7 0.7 copy-start.5
  32.0 6.5 %collective-permute-start.6 = (f32[64,4,6,1]{0,1,3,2:T(4,128)S(1)}, f32[64,4,6,1]{0,1,3,2:T(4,128)S(1)}, u32[]{:S(2)}, u32[]{:S(2)}) collective-permute-start(f32[64,4,6,1]{0,1,3,2:T(4,128)S(1)} %copy.44), channel_id=1, source_target_pairs={{0,1},{1,2},{2,3},{3,4},{4,5},{5,6},{6,7},{7,8},{8,9},{9,10},{10,1... | collective-permute-start | bytes 18440 | tf_op jit(solution)/shard_map/ppermute | solution.py:21
  36.3 5.1 %collective-permute-start.7 = (f32[64,4,6,1]{0,1,3,2:T(4,128)S(1)}, f32[64,4,6,1]{0,1,3,2:T(4,128)S(1)}, u32[]{:S(2)}, u32[]{:S(2)}) collective-permute-start(f32[64,4,6,1]{0,1,3,2:T(4,128)S(1)} %copy.45), channel_id=1, source_target_pairs={{1,0},{2,1},{3,2},{4,3},{5,4},{6,5},{7,6},{8,7},{9,8},{10,9},{11,1... | collective-permute-start | bytes 18440 | tf_op jit(solution)/shard_map/ppermute | solution.py:24
  38.5 4.0 copy-start.1
  42.5 0.9 copy-start.4
  42.5 1.0 copy-start.6
  44.5 7.0 %collective-permute-start.8 = (f32[64,4,1,128]{3,0,2,1:T(8,128)S(1)}, f32[64,4,1,128]{3,0,2,1:T(8,128)S(1)}, u32[]{:S(2)}, u32[]{:S(2)}) collective-permute-start(f32[64,4,1,128]{3,0,2,1:T(8,128)S(1)} %get-tuple-element.240), channel_id=1, source_target_pairs={{0,32},{32,64},{64,96},{96,128},{128,160},{160,192},{192,224},{224... | collective-permute-start | bytes 393224 | tf_op jit(solution)/shard_map/ppermute | solution.py:21
  49.6 6.3 %collective-permute-start.9 = (f32[64,4,1,128]{3,0,2,1:T(8,128)S(1)}, f32[64,4,1,128]{3,0,2,1:T(8,128)S(1)}, u32[]{:S(2)}, u32[]{:S(2)}) collective-permute-start(f32[64,4,1,128]{3,0,2,1:T(8,128)S(1)} %get-tuple-element.241), channel_id=1, source_target_pairs={{32,0},{64,32},{96,64},{128,96},{160,128},{192,160},{224,192},{256... | collective-permute-start | bytes 393224 | tf_op jit(solution)/shard_map/ppermute | solution.py:24
  56.2 7.1 %copy-start.8 = (s32[256]{0:T(256)S(1)}, s32[256]{0:T(256)}, u32[]{:S(2)}) copy-start(s32[256]{0:T(256)} %param.16) | copy-start | bytes 3076
  56.3 12.1 %copy-start.2 = (f32[4,6,130]{2,1,0:T(8,128)S(1)}, f32[4,6,130]{2,1,0:T(8,128)}, u32[]{:S(2)}) copy-start(f32[4,6,130]{2,1,0:T(8,128)} %copy-done.1) | copy-start | bytes 37444
  56.6 6.8 %collective-permute-start.10 = (f32[64,4,6,1]{0,1,3,2:T(4,128)S(1)}, f32[64,4,6,1]{0,1,3,2:T(4,128)S(1)}, u32[]{:S(2)}, u32[]{:S(2)}) collective-permute-start(f32[64,4,6,1]{0,1,3,2:T(4,128)S(1)} %copy.60), channel_id=1, source_target_pairs={{0,1},{1,2},{2,3},{3,4},{4,5},{5,6},{6,7},{7,8},{8,9},{9,10},{10,1... | collective-permute-start | bytes 18440 | tf_op jit(solution)/shard_map/ppermute | solution.py:21
  62.1 5.9 %collective-permute-start.11 = (f32[64,4,6,1]{0,1,3,2:T(4,128)S(1)}, f32[64,4,6,1]{0,1,3,2:T(4,128)S(1)}, u32[]{:S(2)}, u32[]{:S(2)}) collective-permute-start(f32[64,4,6,1]{0,1,3,2:T(4,128)S(1)} %copy.61), channel_id=1, source_target_pairs={{1,0},{2,1},{3,2},{4,3},{5,4},{6,5},{7,6},{8,7},{9,8},{10,9},{11,1... | collective-permute-start | bytes 18440 | tf_op jit(solution)/shard_map/ppermute | solution.py:24
  70.4 4.9 collective-permute-start.12
  73.4 6.3 %collective-permute-start.13 = (f32[64,4,1,128]{3,0,2,1:T(8,128)S(1)}, f32[64,4,1,128]{3,0,2,1:T(8,128)S(1)}, u32[]{:S(2)}, u32[]{:S(2)}) collective-permute-start(f32[64,4,1,128]{3,0,2,1:T(8,128)S(1)} %get-tuple-element.239), channel_id=1, source_target_pairs={{32,0},{64,32},{96,64},{128,96},{160,128},{192,160},{224,192},{256... | collective-permute-start | bytes 393224 | tf_op jit(solution)/shard_map/ppermute | solution.py:24
  80.3 7.1 %collective-permute-start.14 = (f32[64,4,6,1]{0,1,3,2:T(4,128)S(1)}, f32[64,4,6,1]{0,1,3,2:T(4,128)S(1)}, u32[]{:S(2)}, u32[]{:S(2)}) collective-permute-start(f32[64,4,6,1]{0,1,3,2:T(4,128)S(1)} %copy.66), channel_id=1, source_target_pairs={{0,1},{1,2},{2,3},{3,4},{4,5},{5,6},{6,7},{7,8},{8,9},{9,10},{10,1... | collective-permute-start | bytes 18440 | tf_op jit(solution)/shard_map/ppermute | solution.py:21
  85.5 4.7 collective-permute-start.15
  92.6 1.3 copy-start.9
  92.6 1.3 copy-start.10
